TPU v7x, 512 devices: a whole 4x4x16 slice. The times are simulated.
512 devices in a mesh: shot: 128 (over z, x, core), freq: 4 (over y).
Axes of the slice: x: 4, y: 4, z: 16, core: 2. Of those that a mesh axis runs over, the one named last changes fastest.
Arguments:
- traces: float32 [4, 2, 524288], P('freq', None, 'shot'), may hold values from -6 to 6
- trace_slot: int32 [524288], P('shot'), may hold values from 0 to 8191, as said below
- trace_cmp: int32 [524288], P('shot'), may hold values from 0 to 3
- trace_bin: int32 [524288], P('shot'), may hold values from 0 to 511
- prior_weight: float32 [2048, 256], P('shot'), may hold values from 0.5 to 2
Outputs:
- primaries: float32 [4, 2, 524288], P('freq', None, 'shot')
- radon_model: float32 [4, 2, 2048, 256], P('freq', None, 'shot')
Inputs may be any that keep to these rules, and one draw needn't show every extreme that they name: On each index of shot the values are distinct; trace_slot // 16 is the owning shot index of the trace's CMP gather times 4 plus the quarter of that owner's gathers, so at most 16 traces of one index of shot go to one quarter of one owner; in every draw one such quarter receives exactly 16 traces from every index of shot.
All inputs are finite; a program needn't handle non-finite values.
Results may differ from a plain program's by a relative error of at most 0.0085.
Values sent between devices are 32-bit elements; how exact they have to be, the bound alone decides.
A program may use at most 64 MiB of HBM per device.

v0:
```python
import math

import jax
import jax.numpy as jnp
from jax import lax
from jax.sharding import PartitionSpec as P

BINS = 512
Q = 256
CG_STEPS = 8
IRLS = 2


MU_SCALE = 0.5
ENERGY_FLOOR = 0.5
SMALL_EPS = 1e-06


def sent_to_all(value, axis):
    copies = jnp.broadcast_to(value, (lax.axis_size(axis), *value.shape))
    return lax.all_to_all(copies, axis, split_axis=0, concat_axis=0, tiled=True)


def over_copies(value, axis):
    return sent_to_all(value, axis).sum(axis=0)


def radon_table(freq_ids, freq_total):
    nu_value = 0.5 + 0.5 * freq_ids.astype(jnp.float32) / freq_total
    curvature = jnp.arange(Q).astype(jnp.float32) - Q // 8
    offset = (jnp.arange(BINS).astype(jnp.float32) + 0.5) / BINS
    phase = (
        2.0
        * math.pi
        * nu_value[:, None, None]
        * curvature[None, :, None]
        * (offset * offset)[None, None, :]
    )
    return (jnp.cos(phase), -jnp.sin(phase))


def spread(operand, table_part):
    return jnp.einsum("fcq,fqb->fcb", operand, table_part, precision=lax.Precision.HIGHEST)


def collect(operand, table_part):
    return jnp.einsum("fcb,fqb->fcq", operand, table_part, precision=lax.Precision.HIGHEST)


def forward(field, cos_table, sin_table):
    real_part = spread(field[:, 0], cos_table) - spread(field[:, 1], sin_table)
    imag_part = spread(field[:, 1], cos_table) + spread(field[:, 0], sin_table)
    return jnp.stack([real_part, imag_part], axis=1)


def adjoint(binned, cos_table, sin_table):
    real_part = collect(binned[:, 0], cos_table) + collect(binned[:, 1], sin_table)
    imag_part = collect(binned[:, 1], cos_table) - collect(binned[:, 0], sin_table)
    return jnp.stack([real_part, imag_part], axis=1)


def inner_sum(first, second):
    return jnp.sum(first * second, axis=(1, 3))[:, None, :, None]


def conjugate(right_side, counts, weight, cos_table, sin_table):
    damping = MU_SCALE * BINS * weight[None, None]
    fold_map = counts[None, None]
    solution = jnp.zeros_like(right_side)
    residual = right_side
    direction = right_side
    norm_now = inner_sum(residual, residual)
    for cg_step in range(CG_STEPS):
        image_vec = (
            adjoint(fold_map * forward(direction, cos_table, sin_table), cos_table, sin_table)
            + damping * direction
        )
        step_size = norm_now / inner_sum(direction, image_vec)
        solution = solution + step_size * direction
        residual = residual - step_size * image_vec
        norm_next = inner_sum(residual, residual)
        direction = residual + norm_next / norm_now * direction
        norm_now = norm_next
    return solution


def reweigh(energy):
    average = jnp.mean(energy, axis=1, keepdims=True)
    return (average + SMALL_EPS) / (energy + ENERGY_FLOOR * average + SMALL_EPS)


def per_device(traces, trace_slot, trace_cmp, trace_bin, prior_weight):
    freq_dev = traces.shape[0]
    trace_dev = traces.shape[2]
    shot_count = lax.axis_size("shot")
    freq_count = lax.axis_size("freq")
    cmp_dev = prior_weight.shape[0]
    cmp_quarter = cmp_dev // freq_count
    cap_quarter = 2 * trace_dev // (shot_count * freq_count)
    per_owner = freq_count * cap_quarter
    slot_total = shot_count * per_owner
    outgoing = jnp.zeros((freq_dev, 2, slot_total), jnp.float32).at[:, :, trace_slot].set(traces)
    slot_labels = (
        jnp.zeros((slot_total,), jnp.int32).at[trace_slot].set(1 + trace_cmp * BINS + trace_bin)
    )
    outgoing = outgoing.reshape(freq_dev, 2, shot_count, per_owner)
    slot_labels = slot_labels.reshape(1, 1, shot_count, per_owner)
    arrived, slot_codes = (
        lax.all_to_all(outgoing, "shot", split_axis=2, concat_axis=2, tiled=True),
        lax.all_to_all(slot_labels, "shot", split_axis=2, concat_axis=2, tiled=True),
    )
    quarter_index = (jnp.arange(per_owner, dtype=jnp.int32) // cap_quarter)[None, :]
    freq_ids = lax.axis_index("freq") * freq_dev + jnp.arange(freq_dev, dtype=jnp.int32)
    weight = prior_weight
    slot_codes = slot_codes[0, 0]
    occupied = slot_codes > 0
    cmp_within = (slot_codes - 1) // BINS
    cell_index = (quarter_index * cmp_quarter + cmp_within) * BINS + (slot_codes - 1) % BINS
    cell_index = jnp.where(occupied, cell_index, cmp_dev * BINS).reshape(-1)
    freq_local = arrived.shape[0]
    binned = (
        jnp.zeros((freq_local * 2, cmp_dev * BINS + 1), jnp.float32)
        .at[:, cell_index]
        .add(arrived.reshape(freq_local * 2, -1))
    )
    binned = binned[:, :-1].reshape(freq_local, 2, cmp_dev, BINS)
    counts = (
        jnp.zeros((cmp_dev * BINS + 1,), jnp.float32)
        .at[cell_index]
        .add(occupied.reshape(-1).astype(jnp.float32))
    )
    counts = counts[:-1].reshape(cmp_dev, BINS)
    cos_table, sin_table = radon_table(freq_ids, freq_dev * freq_count)
    right_side = adjoint(binned, cos_table, sin_table)
    radon_model = right_side
    for irls_pass in range(IRLS):
        if irls_pass > 0:
            energy = jnp.sum(radon_model * radon_model, axis=(0, 1))
            energy = over_copies(energy, "freq")
            weight = reweigh(energy)
        radon_model = conjugate(right_side, counts, weight, cos_table, sin_table)
    multiple_mask = (jnp.arange(Q) >= Q // 4).astype(jnp.float32)
    predicted = forward(radon_model * multiple_mask, cos_table, sin_table).reshape(
        freq_local, 2, cmp_dev * BINS
    )
    predicted = jnp.concatenate([predicted, jnp.zeros((freq_local, 2, 1), jnp.float32)], axis=2)
    returned = predicted[:, :, cell_index].reshape(freq_local, 2, shot_count, -1)
    arrived_back = lax.all_to_all(returned, "shot", split_axis=2, concat_axis=2, tiled=True)
    arrived_back = arrived_back.reshape(freq_dev, 2, slot_total)
    primaries = traces - arrived_back[:, :, trace_slot]
    return (primaries, radon_model)


def solution(mesh):
    return jax.shard_map(
        per_device,
        mesh=mesh,
        in_specs=(P("freq", None, "shot"), P("shot"), P("shot"), P("shot"), P("shot", None)),
        out_specs=(P("freq", None, "shot"), P("freq", None, "shot", None)),
        check_vma=False,
    )
```

profile of v0, /device:TPU:1, one launch (start us, length us, event | category | flops | bytes accessed | tf_op | source)
XLA Modules:
  0.0 382.0 jit_solution(3050658304022552669)
XLA Ops:
  0.6 0.8 broadcast_clamp_fusion.1
  1.4 15.5 %scatter_custom_fusion = s32[8192]{0:T(1024)S(1)} fusion(s32[4096]{0:T(1024)S(1)} %get-tuple-element.45, s32[4096]{0:T(1024)S(1)} %get-tuple-element.50, s32[]{:T(128)} %constant.78.clone.1), kind=kCustom, calls=%fused_computation.518 | custom fusion | bytes 32772 | tf_op jit(solution)/shard_map/scatter | solution.py:104
  17.0 0.7 reshape.10899
  17.7 20.4 %all-to-all-start = ((s32[1,1,128,64]{3,1,0,2:T(1,128)}), s32[1,1,128,64]{3,1,0,2:T(1,128)S(1)}, u32[]{:S(2)}, u32[]{:S(2)}) async-start(s32[1,1,128,64]{3,1,0,2:T(1,128)} %bitcast), calls=%async_computation | async-start | bytes 131072 | tf_op jit(solution)/shard_map/all_to_all | solution.py:110
  38.1 0.7 broadcast_multiply_fusion.1
  38.8 15.4 %fusion.66 = (f32[1,256,1,1,1,1,512]{6,5,4,3,2,1,0:T(1,128)S(1)}, f32[1,256,1,1,1,1,512]{6,5,4,3,2,1,0:T(1,128)S(1)}) fusion(f32[512]{0:T(512)S(1)} %multiply_multiply_fusion, f32[256]{0:T(256)S(1)} %add_multiply_fusion), kind=kLoop, calls=%fused_computation.142 | loop fusion | flops 262144 | bytes 1051648 | tf_op jit(solution)/shard_map/neg | solution.py:39
  54.3 1.4 copy.42
  55.7 12.8 %scatter_custom_fusion.1 = f32[2,8192]{0,1:T(8,128)} fusion(s32[4096]{0:T(1024)S(1)} %get-tuple-element.45, f32[4096,2]{1,0:T(8,128)S(1)} %copy.42, f32[]{:T(128)} %constant.42.clone.1), kind=kCustom, calls=%fused_computation.10 | custom fusion | bytes 65540 | tf_op jit(solution)/shard_map/scatter | solution.py:102
  68.5 3.0 copy.43
  71.5 0.8 reshape.11051
  72.3 16.4 %all-to-all-start.1 = ((f32[128,1,128]{2,1,0:T(1,128)}), f32[128,1,128]{2,1,0:T(1,128)S(1)}, u32[]{:S(2)}, u32[]{:S(2)}) async-start(f32[128,1,128]{2,1,0:T(1,128)} %reshape.11051), calls=%async_computation.1 | async-start | bytes 131072 | tf_op jit(solution)/shard_map/all_to_all | solution.py:109
  89.9 43.2 %scatter_custom_fusion.3 = f32[8193]{0:T(1024)S(1)} fusion(s32[8192]{0:T(1024)S(1)} %bitcast.688, f32[8192]{0:T(1024)S(1)} %reshape.11018, f32[]{:T(128)} %constant.42.clone.1), kind=kCustom, calls=%fused_computation.482 | custom fusion | flops 8192 | bytes 32776 | tf_op jit(solution)/shard_map/scatter-add | solution.py:130
  133.7 0.8 reduce.42
  134.8 2.7 copy.45
  137.4 46.5 %scatter_custom_fusion.2 = f32[2,8193]{0,1:T(8,128)} fusion(s32[8192]{0:T(1024)S(1)} %bitcast.689, f32[8192,2]{1,0:T(8,128)} %copy.45, f32[]{:T(128)} %constant.42.clone.1), kind=kCustom, calls=%fused_computation.7 | custom fusion | flops 16384 | bytes 66056 | tf_op jit(solution)/shard_map/scatter-add | solution.py:124
  183.9 2.2 slice-done
  186.1 4.7 %fusion.405 = (f32[1,1,16,512]{1,3,2,0:T(8,128)}, f32[1,1,16,512]{1,3,2,0:T(8,128)}) fusion(f32[1,2,16,512]{1,3,2,0:T(8,128)S(1)} %bitcast.650), kind=kLoop, calls=%fused_computation.657 | loop fusion | bytes 131072 | tf_op jit(solution)/shard_map/slice | solution.py:57
  190.8 2.8 copy.55
  193.6 3.2 copy.56
  197.9 0.5 convolution_add_fusion.31
  198.4 2.1 fusion.65
  201.1 2.1 fusion.64
  203.2 2.1 fusion.33
  205.3 2.2 fusion.32
  208.6 0.5 fusion.63
  210.8 0.5 fusion.31
  216.9 0.5 fusion.59
  221.5 0.5 fusion.56
  225.0 0.5 fusion.55
  228.5 0.9 fusion.208
  238.8 0.6 broadcast_in_dim.19
  239.5 4.2 %all-to-all-start.2 = ((f32[4,16,256]{2,1,0:T(8,128)}), f32[4,16,256]{2,1,0:T(8,128)S(1)}, u32[]{:S(2)}, u32[]{:S(2)}) async-start(f32[4,16,256]{2,1,0:T(8,128)} %broadcast_in_dim.19), calls=%async_computation.2 | async-start | bytes 131072 | tf_op jit(solution)/shard_map/all_to_all | solution.py:21
  243.7 4.5 %all-to-all-done.2 = f32[4,16,256]{2,1,0:T(8,128)S(1)} async-done(((f32[4,16,256]{2,1,0:T(8,128)}), f32[4,16,256]{2,1,0:T(8,128)S(1)}, u32[]{:S(2)}, u32[]{:S(2)}) %all-to-all-start.2) | async-done | bytes 65568 | tf_op jit(solution)/shard_map/all_to_all | solution.py:21
  266.1 0.5 fusion.8
  277.0 0.7 broadcast_multiply_fusion
  279.4 2.7 copy.48
  282.1 3.7 pad_bitcast_fusion
  285.7 30.1 %gather_fusion = f32[8192,2]{1,0:T(8,128)} fusion(f32[2,8193]{0,1:T(8,128)} %pad_bitcast_fusion, s32[8192]{0:T(1024)S(1)} %broadcast_clamp_fusion), kind=kCustom, calls=%fused_computation | custom fusion | bytes 163840 | tf_op jit(solution)/shard_map/gather | solution.py:147
  315.9 3.0 copy.49
  318.8 0.8 reshape.11053
  319.6 21.4 %all-to-all-start.3 = ((f32[128,1,128]{2,1,0:T(1,128)}), f32[128,1,128]{2,1,0:T(1,128)S(1)}, u32[]{:S(2)}, u32[]{:S(2)}) async-start(f32[128,1,128]{2,1,0:T(1,128)} %reshape.11053), calls=%async_computation.3 | async-start | bytes 131072 | tf_op jit(solution)/shard_map/all_to_all | solution.py:148
  341.1 0.6 copy.51
  341.7 14.2 %all-to-all-done.3 = f32[128,1,128]{2,1,0:T(1,128)S(1)} async-done(((f32[128,1,128]{2,1,0:T(1,128)}), f32[128,1,128]{2,1,0:T(1,128)S(1)}, u32[]{:S(2)}, u32[]{:S(2)}) %all-to-all-start.3) | async-done | bytes 65568 | tf_op jit(solution)/shard_map/all_to_all | solution.py:148
  355.9 0.8 reduce.43
  356.8 2.7 copy.50
  359.6 16.3 %gather_fusion.1 = f32[4096,2]{1,0:T(8,128)} fusion(f32[2,8192]{0,1:T(8,128)} %bitcast.652, s32[4096]{0:T(1024)S(1)} %get-tuple-element.44), kind=kCustom, calls=%fused_computation.1 | custom fusion | bytes 81920 | tf_op jit(solution)/shard_map/gather | solution.py:150
  375.8 3.1 bitcast_subtract_fusion
  378.9 2.8 copy.52
  (238 shorter events, 61.1 us)
Async XLA Ops:
  17.7 54.6 %all-to-all-start = ((s32[1,1,128,64]{3,1,0,2:T(1,128)}), s32[1,1,128,64]{3,1,0,2:T(1,128)S(1)}, u32[]{:S(2)}, u32[]{:S(2)}) async-start(s32[1,1,128,64]{3,1,0,2:T(1,128)} %bitcast), calls=%async_computation | async-start | bytes 131072 | tf_op jit(solution)/shard_map/all_to_all | solution.py:110
  72.3 60.9 %all-to-all-start.1 = ((f32[128,1,128]{2,1,0:T(1,128)}), f32[128,1,128]{2,1,0:T(1,128)S(1)}, u32[]{:S(2)}, u32[]{:S(2)}) async-start(f32[128,1,128]{2,1,0:T(1,128)} %reshape.11051), calls=%async_computation.1 | async-start | bytes 131072 | tf_op jit(solution)/shard_map/all_to_all | solution.py:109
  183.9 2.2 slice-start
  239.5 8.7 %all-to-all-start.2 = ((f32[4,16,256]{2,1,0:T(8,128)}), f32[4,16,256]{2,1,0:T(8,128)S(1)}, u32[]{:S(2)}, u32[]{:S(2)}) async-start(f32[4,16,256]{2,1,0:T(8,128)} %broadcast_in_dim.19), calls=%async_computation.2 | async-start | bytes 131072 | tf_op jit(solution)/shard_map/all_to_all | solution.py:21
  285.7 55.3 %copy-start = (f32[1,2,4096]{2,1,0:T(2,128)S(1)}, f32[1,2,4096]{2,1,0:T(2,128)}, u32[]{:S(2)}) copy-start(f32[1,2,4096]{2,1,0:T(2,128)} %param.5) | copy-start | bytes 98308
  319.6 36.3 %all-to-all-start.3 = ((f32[128,1,128]{2,1,0:T(1,128)}), f32[128,1,128]{2,1,0:T(1,128)S(1)}, u32[]{:S(2)}, u32[]{:S(2)}) async-start(f32[128,1,128]{2,1,0:T(1,128)} %reshape.11053), calls=%async_computation.3 | async-start | bytes 131072 | tf_op jit(solution)/shard_map/all_to_all | solution.py:148
where the time goes:
time: 390 us; the launch traced here: 382 us
  other arithmetic  120 us (31%)
  local copies, waits for them, and re-layouts  114 us (29%)
  matrix products  65.3 us (17%)
  starting transfers between devices  62.4 us (16%)
  waiting for transfers between devices  18.6 us (5%)
    scatter-add x1, other arithmetic, per_device(): binned = jnp.zeros((freq_local * 2, cmp_dev * BINS + 1), jnp.float32).at[...  46.5 us
    scatter-add x1, other arithmetic, per_device(): counts = jnp.zeros((cmp_dev * BINS + 1,), jnp.float32).at[cell_index].add...  43.2 us
    dot_general x64, matrix products, collect(): jnp.einsum('fcb,fqb->fcq', operand, table_part, precision=lax.Precision.H...  34 us
    dot_general x64, matrix products, spread(): jnp.einsum('fcq,fqb->fcb', operand, table_part, precision=lax.Precision.H...  31.3 us
    gather x1, local copies, waits for them, and re-layouts, per_device(): predicted[:, :, cell_index].reshape(freq_local, 2, shot_count, -1)  30.1 us
    all_to_all x1, starting transfers between devices, per_device(): lax.all_to_all(returned, 'shot', split_axis=2, concat_axis=2, tiled=True)  21.4 us
    all_to_all x1, starting transfers between devices, per_device(): lax.all_to_all(slot_labels, 'shot', split_axis=2, concat_axis=2, tiled=True)  20.4 us
    all_to_all x1, starting transfers between devices, per_device(): lax.all_to_all(outgoing, 'shot', split_axis=2, concat_axis=2, tiled=True)  16.4 us
  transfers between devices with their start and end apart: 4, of which 2 were waited for; matrix products, arithmetic and copies ran while one was open for 21% of the time, Pallas kernels for 0%

commit v1 on v0

v1 whole, which is shorter than its diff:
```python
import math

import jax
import jax.numpy as jnp
from jax import lax
from jax.experimental import pallas as pl
from jax.experimental.pallas import tpu as pltpu
from jax.sharding import PartitionSpec as P

BINS = 512
Q = 256
HALF = 128
CG_STEPS = 8
KEPT = 3
MU_SCALE = 0.5
ENERGY_FLOOR = 0.5
SMALL_EPS = 1e-06

NZ = 16
NU = 8
NF = 4
CMP = 16
TRACES = 4096
GROUP = 1024
MESH = pl.DeviceIdType.MESH
F32 = jnp.float32
BF16 = jnp.bfloat16

NN = (((1,), (0,)), ((), ()))
NT = (((1,), (1,)), ((), ()))


def mxu(a, b, dims=NN):
    return lax.dot_general(a, b, dims, preferred_element_type=F32)


def split(v, pieces=2):
    out = [v.astype(BF16)]
    for _ in range(pieces - 1):
        v = v - out[-1].astype(F32)
        out.append(v.astype(BF16))
    return out


def reverse_lanes(v, flip):
    n = v.shape[0]
    out = mxu(jnp.concatenate(split(v, 3), axis=0), flip)
    return out[:n] + out[n : 2 * n] + out[2 * n :]


def sincos(k):
    quadrant = (k + (1 << 21)) >> 22
    rem = (k - (quadrant << 22)).astype(F32)
    t = rem * (2.0 * math.pi / (1 << 24))
    u = t * t
    s = t + t * u * (-1.0 / 6 + u * (1.0 / 120 + u * (-1.0 / 5040 + u * (1.0 / 362880))))
    c = 1.0 + u * (-0.5 + u * (1.0 / 24 + u * (-1.0 / 720 + u * (1.0 / 40320 + u * (-1.0 / 3628800)))))
    quadrant = quadrant & 3
    odd = (quadrant & 1) == 1
    cos = jnp.where(odd, s, c)
    sin = jnp.where(odd, c, s)
    cos = jnp.where((quadrant == 1) | (quadrant == 2), -cos, cos)
    sin = jnp.where(quadrant >= 2, -sin, sin)
    return cos, sin


def kernel(
    traces_hbm, slot_hbm, cmp_hbm, bin_hbm, weight_hbm, primaries, radon_model,
    traces, slot_in, cmp_in, bin_in, weight_in, in_sems,
    dest_hot, trace_hot, slot_low, slot_hot, row_h, row_s,
    table, table_low, table_t, table_t_low, counts_ref,
    send_a, recv_a, pair_code, recv_v, recv_c, energy_own, energy_all, send_r, recv_r, recv_t,
    a_send, a_recv, b_send, b_recv, c_send, c_recv, e_send, e_recv, r_send, r_recv, t_send, t_recv,
):
    inputs = [
        pltpu.make_async_copy(source, target, in_sems.at[i])
        for i, (source, target) in enumerate(
            (
                (slot_hbm, slot_in),
                (traces_hbm, traces),
                (bin_hbm, bin_in),
                (cmp_hbm, cmp_in),
                (weight_hbm, weight_in),
            )
        )
    ]
    for copy in inputs:
        copy.start()

    shot = lax.axis_index("shot")
    f = lax.axis_index("freq")
    z = shot // NU
    x_core = lax.rem(shot, NU)
    core = lax.rem(x_core, 2)
    u = core * 4 + x_core // 2

    def shot_of(z_at, u_at):
        return z_at * NU + lax.rem(u_at, 4) * 2 + u_at // 4

    barrier = pltpu.get_barrier_semaphore()
    for k in range(1, NU):
        peer = shot_of(z, lax.rem(u + k, NU))
        pl.semaphore_signal(barrier, inc=1, device_id={"shot": peer}, device_id_type=MESH)
    for k in range(1, NZ):
        peer = shot_of(lax.rem(z + k, NZ), u)
        pl.semaphore_signal(barrier, inc=1, device_id={"shot": peer}, device_id_type=MESH)
    for k in range(1, NF):
        pl.semaphore_signal(barrier, inc=1, device_id={"freq": lax.rem(f + k, NF)}, device_id_type=MESH)

    lane = lax.broadcasted_iota(jnp.int32, (8, 128), 1)
    sub64 = lax.broadcasted_iota(jnp.int32, (64, 128), 0)
    sub128 = lax.broadcasted_iota(jnp.int32, (128, 128), 0)

    for copy in inputs:
        copy.wait()

    @pl.loop(0, TRACES // GROUP)
    def _(step):
        rows = pl.ds(pl.multiple_of(step * 8, 8), 8)
        slot, bins = slot_in[rows, :], bin_in[rows, :]
        dest = (((slot >> 6) & 1) * 4 + ((slot >> 7) & 3)) * NZ + (slot >> 9)
        within = slot & 63
        row_s[rows, :] = within
        high = (bins >> 7) * 16 + ((slot >> 4) & 3) * 4 + cmp_in[rows, :] + 1
        low = bins & 127
        high, low = high.astype(F32), low.astype(F32)
        for i in range(8):
            lanes = pl.ds(pl.multiple_of(step * GROUP + i * 128, 128), 128)
            re_h, re_l = split(traces[0, 0:1, lanes])
            im_h, im_l = split(traces[0, 1:2, lanes])
            dest_hot[:, lanes] = jnp.where(sub128 == dest[i : i + 1], 1.0, 0.0).astype(BF16)
            mask = sub64 == within[i : i + 1]
            for j, piece in enumerate((re_h, im_h, re_l, im_l, high[i : i + 1], low[i : i + 1])):
                trace_hot[64 * j : 64 * (j + 1), lanes] = jnp.where(mask, piece.astype(F32), 0.0).astype(BF16)

    placed = mxu(dest_hot[...], trace_hot[...], NT)
    values = placed[:, 0:128] + placed[:, 128:256]
    codes = placed[:, 256:384]
    turned = pltpu.roll(codes, 64, 1)
    lane_full = lax.broadcasted_iota(jnp.int32, (128, 128), 1)
    codes = jnp.where(lane_full < 64, 128.0 * codes + turned, 128.0 * turned + codes)
    codes = jnp.where(lane_full // 64 == core, codes, 0.0)
    send_a[:, 0] = values.reshape(NU, NZ, 128)
    send_a[:, 1] = codes.reshape(NU, NZ, 128)

    pl.semaphore_wait(barrier, NU + NZ + NF - 3)

    def copy_a(k):
        peer = lax.rem(u + k, NU)
        return pltpu.make_async_remote_copy(
            send_a.at[peer], recv_a.at[u], a_send.at[k], a_recv.at[k],
            device_id={"shot": shot_of(z, peer)}, device_id_type=MESH,
        )

    for k in range(1, NU):
        copy_a(k).start()
    recv_a[u] = send_a[u]

    factor = math.sqrt(2.0)
    odd_m = 2 * lax.broadcasted_iota(jnp.int32, (64, HALF), 1) + 1

    @pl.loop(0, BINS // 64)
    def _(step):
        b = 2 * (lax.broadcasted_iota(jnp.int32, (64, HALF), 0) + step * 64) + 1
        cos, sin = sincos((4 + f) * odd_m * b * b)
        high, low = split(factor * cos)
        rows = pl.ds(pl.multiple_of(step * 64, 64), 64)
        table[rows, 0:HALF] = high
        table_low[rows, 0:HALF] = low
        high, low = split(factor * sin)
        table[rows, HALF:Q] = high
        table_low[rows, HALF:Q] = low

    for k in range(1, NU):
        copy_a(k).wait_recv()
    for i in range(4):
        pair_code[i] = recv_a[i, 1] + recv_a[i + 4, 1]

    def copies_b(k):
        there = lax.rem(z + k, NZ)
        peer = {"shot": shot_of(there, u)}
        return (
            pltpu.make_async_remote_copy(
                recv_a.at[:, 0, there], recv_v.at[z], b_send.at[k], b_recv.at[k],
                device_id=peer, device_id_type=MESH,
            ),
            pltpu.make_async_remote_copy(
                pair_code.at[:, there], recv_c.at[z], c_send.at[k], c_recv.at[k],
                device_id=peer, device_id_type=MESH,
            ),
        )

    for k in (8, 7, 9, 6, 10, 5, 11, 4, 12, 3, 13, 2, 14, 1, 15):
        for copy in copies_b(k):
            copy.start()
    recv_v[z] = recv_a[:, 0, z]
    recv_c[z] = pair_code[:, z]

    odd_row = 2 * lax.broadcasted_iota(jnp.int32, (64, 128), 0) + 1

    @pl.loop(0, BINS // 128)
    def _(step):
        b = 2 * (lax.broadcasted_iota(jnp.int32, (64, 128), 1) + step * 128) + 1
        lanes = pl.ds(pl.multiple_of(step * 128, 128), 128)
        for part in range(2):
            rows = slice(part * 64, part * 64 + 64)
            cos, sin = sincos((4 + f) * (odd_row + part * 128) * b * b)
            high, low = split(factor * cos)
            table_t[rows, lanes] = high
            table_t_low[rows, lanes] = low
            rows = slice(HALF + part * 64, HALF + part * 64 + 64)
            high, low = split(factor * sin)
            table_t[rows, lanes] = high
            table_t_low[rows, lanes] = low

    b = 2 * lax.broadcasted_iota(jnp.int32, (1, BINS), 1) + 1
    shift_cos, shift_sin = sincos((4 + f) * (191 * b * b))
    flip = jnp.where(sub128 + lane_full == 127, 1.0, 0.0).astype(BF16)
    weight = weight_in[...]
    w_plus, w_minus = weight[:, HALF:], reverse_lanes(weight[:, :HALF], flip)

    lane4 = lax.broadcasted_iota(jnp.int32, (4, 128), 1)

    def bin_step(step, below, above, total):
        rows = pl.ds(pl.multiple_of(step * 8, 8), 8)
        re, im, code = [], [], []
        for at in (below, above):
            first, second = recv_v[at, 0:4], recv_v[at, 4:8]
            re.append(jnp.where(lane4 < 64, first, pltpu.roll(second, 64, 1)))
            im.append(jnp.where(lane4 < 64, pltpu.roll(first, 64, 1), second))
            code.append(recv_c[at])
        re, im = jnp.concatenate(re, axis=0), jnp.concatenate(im, axis=0)
        code = jnp.concatenate(code, axis=0).astype(jnp.int32)
        h, low = (code >> 7) - 1, code & 127
        row_h[rows, :] = h
        pieces = [p.astype(F32) for v in (re, im) for p in split(v)]
        for i in range(8):
            lanes = pl.ds(pl.multiple_of(step * GROUP + i * 128, 128), 128)
            here = slice(i * 128, i * 128 + 128)
            slot_low[:, lanes] = jnp.where(sub128 == low[i : i + 1], 1.0, 0.0).astype(BF16)
            mask = sub64 == h[i : i + 1]
            for j, piece in enumerate(pieces):
                slot_hot[64 * j : 64 * (j + 1), here] = jnp.where(mask, piece[i : i + 1], 0.0).astype(BF16)
            slot_hot[256:320, here] = jnp.where(mask, 1.0, 0.0).astype(BF16)
        lanes = pl.ds(pl.multiple_of(step * GROUP, 128), GROUP)
        return total + mxu(slot_hot[...], slot_low[:, lanes], NT)

    def bin_pair(step, total):
        for k in (step + 1, NZ - 1 - step):
            for copy in copies_b(k):
                copy.wait_recv()
        return bin_step(step, lax.rem(z + NZ - 1 - step, NZ), lax.rem(z + step + 1, NZ), total)

    binned = lax.fori_loop(0, 7, bin_pair, jnp.zeros((320, 128), F32))
    for copy in copies_b(8):
        copy.wait_recv()
    binned = bin_step(7, z, lax.rem(z + 8, NZ), binned)

    def by_bin(rows):
        return jnp.concatenate([rows[16 * i : 16 * i + 16] for i in range(4)], axis=1)

    g_re = by_bin(binned[0:64] + binned[64:128])
    g_im = by_bin(binned[128:192] + binned[192:256])
    counts_ref[...] = by_bin(binned[256:320])

    def product(v, high, low):
        n = v.shape[0]
        v_high, v_low = split(v)
        main = mxu(jnp.concatenate([v_high, v_low], axis=0), high)
        return main[:n] + (main[n:] + mxu(v_high, low))

    def forward(v):
        return product(v, table_t[...], table_t_low[...])

    def adjoint(g):
        return product(g, table[...], table_low[...])

    right_side = adjoint(
        jnp.concatenate([shift_cos * g_re - shift_sin * g_im, shift_cos * g_im + shift_sin * g_re], axis=0)
    )

    def inner(a, b):
        p = a * b
        return jnp.sum(p[:CMP] + p[CMP:], axis=1, keepdims=True)

    def both_parts(v):
        return jnp.concatenate([v, v], axis=0)

    def undamped(v):
        return adjoint(forward(v) * both_parts(counts_ref[...]))

    first_image = undamped(right_side)

    def solve(w_plus, w_minus):
        scale = 0.5 * MU_SCALE * BINS
        even, odd = scale * (w_plus + w_minus), scale * (w_plus - w_minus)

        def damp(v):
            s_re, s_im, t_re, t_im = v[:CMP, :HALF], v[CMP:, :HALF], v[:CMP, HALF:], v[CMP:, HALF:]
            return jnp.concatenate(
                [
                    jnp.concatenate([even * s_re - odd * t_im, even * t_re + odd * s_im], axis=1),
                    jnp.concatenate([even * s_im + odd * t_re, even * t_im - odd * s_re], axis=1),
                ],
                axis=0,
            )

        def image_of(direction):
            return undamped(direction) + damp(direction)

        def project(image, past, scales):
            out = image
            for old, scale in zip(past, scales):
                swapped = swap(old)
                along = both_parts(inner(old, image) * scale)
                across = both_parts(inner(swapped, image) * scale)
                out = out - (along * old + across * swapped)
            return out

        def swap(v):
            return jnp.concatenate([-v[CMP:], v[:CMP]], axis=0)

        def cg_step(state, past, scales, own):
            answer, residual, direction, norm_now = state
            image = first_image + damp(direction) if own and not past else image_of(direction)
            step_size = both_parts(norm_now / inner(direction, image))
            kept = project(image, past, scales)
            if own:
                swapped = swap(residual)
                kept = kept - both_parts(inner(swapped, image) / norm_now) * swapped
            answer = answer + step_size * direction
            residual = residual - step_size * kept
            norm_next = inner(residual, residual)
            direction = residual + both_parts(norm_next / norm_now) * direction
            return answer, residual, direction, norm_next

        state = (jnp.zeros_like(right_side), right_side, right_side, inner(right_side, right_side))
        past, scales = [], []
        for _ in range(KEPT):
            residual, norm = state[1], state[3]
            state = cg_step(state, past, scales, True)
            past.append(residual)
            scales.append(1.0 / norm)
        state = lax.fori_loop(
            KEPT, CG_STEPS - 1, lambda _, state: cg_step(state, past, scales, False), state
        )
        answer, _, direction, norm_now = state
        return answer + both_parts(norm_now / inner(direction, image_of(direction))) * direction

    def to_curvatures(v):
        root = math.sqrt(0.5)
        s_re, s_im, t_re, t_im = v[:CMP, :HALF], v[CMP:, :HALF], v[:CMP, HALF:], v[CMP:, HALF:]
        plus = root * (s_re - t_im), root * (s_im + t_re)
        minus = root * (s_re + t_im), root * (s_im - t_re)
        return plus, minus

    answer = solve(w_plus, w_minus)
    plus, minus = to_curvatures(answer)
    energy_own[:, :HALF] = plus[0] * plus[0] + plus[1] * plus[1]
    energy_own[:, HALF:] = minus[0] * minus[0] + minus[1] * minus[1]

    def copy_e(k):
        peer = lax.rem(f + k, NF)
        return pltpu.make_async_remote_copy(
            energy_own, energy_all.at[f], e_send.at[k], e_recv.at[k],
            device_id={"freq": peer}, device_id_type=MESH,
        )

    for k in (2, 1, 3):
        copy_e(k).start()
    energy_all[f] = energy_own[...]
    for k in (1, 3, 2):
        copy_e(k).wait_recv()
    energy = (energy_all[0] + energy_all[1]) + (energy_all[2] + energy_all[3])
    average = jnp.sum(energy, axis=1, keepdims=True) * (1.0 / Q)
    weight = (average + SMALL_EPS) / (energy + ENERGY_FLOOR * average + SMALL_EPS)
    answer = solve(weight[:, :HALF], weight[:, HALF:])
    plus, minus = to_curvatures(answer)

    root = math.sqrt(0.5)
    keep = lax.broadcasted_iota(jnp.int32, (CMP, HALF), 1) < 64
    low_re, low_im = jnp.where(keep, minus[0], 0.0), jnp.where(keep, minus[1], 0.0)
    masked = jnp.concatenate(
        [
            jnp.concatenate([root * (plus[0] + low_re), root * (plus[1] - low_im)], axis=1),
            jnp.concatenate([root * (plus[1] + low_im), root * (low_re - plus[0])], axis=1),
        ],
        axis=0,
    )
    field = forward(masked)
    p_re = shift_cos * field[:CMP] + shift_sin * field[CMP:]
    p_im = shift_cos * field[CMP:] - shift_sin * field[:CMP]
    predicted = jnp.concatenate(
        [p[:, 128 * i : 128 * i + 128] for p in (p_re, p_im) for i in range(4)], axis=0
    )
    predicted = jnp.concatenate(split(predicted), axis=1)

    def copy_r(k):
        there = lax.rem(z + k, NZ)
        return pltpu.make_async_remote_copy(
            send_r.at[there], recv_r.at[z], r_send.at[k], r_recv.at[k],
            device_id={"shot": shot_of(there, u)}, device_id_type=MESH,
        )

    lane8 = lax.broadcasted_iota(jnp.int32, (8, 128), 1)

    def predict(step, below, above):
        rows = pl.ds(pl.multiple_of(step * 8, 8), 8)
        low = slot_low[:, pl.ds(pl.multiple_of(step * GROUP, 128), GROUP)]
        found = mxu(predicted, jnp.concatenate([low, low], axis=0))
        h = row_h[rows, :]
        got_re, got_im = [], []
        for i in range(8):
            mask = sub64 == h[i : i + 1]
            here = slice(i * 128, i * 128 + 128)
            got_re.append(jnp.sum(jnp.where(mask, found[:64, here], 0.0), axis=0, keepdims=True))
            got_im.append(jnp.sum(jnp.where(mask, found[64:, here], 0.0), axis=0, keepdims=True))
        got_re, got_im = jnp.concatenate(got_re, axis=0), jnp.concatenate(got_im, axis=0)
        first = jnp.where(lane8 < 64, got_re, pltpu.roll(got_im, 64, 1))
        second = jnp.where(lane8 < 64, pltpu.roll(got_re, 64, 1), got_im)
        for i, at in enumerate((below, above)):
            send_r[at, 0:4] = first[4 * i : 4 * i + 4]
            send_r[at, 4:8] = second[4 * i : 4 * i + 4]

    predict(7, z, lax.rem(z + 8, NZ))
    copy_r(8).start()
    recv_r[z] = send_r[z]

    @pl.loop(0, 7)
    def _(back):
        step = 6 - back
        predict(step, lax.rem(z + NZ - 1 - step, NZ), lax.rem(z + step + 1, NZ))
        copy_r(NZ - 1 - step).start()
        copy_r(step + 1).start()

    for part in range(2):
        radon_model[0, part, :, 0:HALF] = reverse_lanes(minus[part], flip)
        radon_model[0, part, :, HALF:Q] = plus[part]

    for k in range(1, NZ):
        copy_r(k).wait_recv()

    def copy_t(k):
        peer = lax.rem(u + k, NU)
        return pltpu.make_async_remote_copy(
            recv_r.at[:, peer], recv_t.at[u], t_send.at[k], t_recv.at[k],
            device_id={"shot": shot_of(z, peer)}, device_id_type=MESH,
        )

    for k in range(1, NU):
        copy_t(k).start()
    recv_t[u] = recv_r[:, u]
    for k in range(1, NU):
        copy_t(k).wait_recv()

    by_slot = jnp.concatenate(split(recv_t[...].reshape(128, 128).T), axis=1)

    @pl.loop(0, TRACES // GROUP)
    def _(step):
        rows = pl.ds(pl.multiple_of(step * 8, 8), 8)
        hot = dest_hot[:, pl.ds(pl.multiple_of(step * GROUP, 128), GROUP)]
        found = mxu(by_slot, jnp.concatenate([hot, hot], axis=0))
        within = row_s[rows, :]
        for i in range(8):
            mask = sub64 == within[i : i + 1]
            here = slice(i * 128, i * 128 + 128)
            lanes = pl.ds(pl.multiple_of(step * GROUP + i * 128, 128), 128)
            got = jnp.sum(jnp.where(mask, found[:64, here], 0.0), axis=0, keepdims=True)
            primaries[0, 0:1, lanes] = traces[0, 0:1, lanes] - got
            got = jnp.sum(jnp.where(mask, found[64:, here], 0.0), axis=0, keepdims=True)
            primaries[0, 1:2, lanes] = traces[0, 1:2, lanes] - got

    for k in range(1, NU):
        copy_a(k).wait_send()
        copy_t(k).wait_send()
    for k in range(1, NZ):
        for copy in copies_b(k):
            copy.wait_send()
        copy_r(k).wait_send()
    for k in range(1, NF):
        copy_e(k).wait_send()


def per_device(traces, trace_slot, trace_cmp, trace_bin, prior_weight):
    rows = TRACES // 128
    vmem = pl.BlockSpec(memory_space=pltpu.VMEM)
    dma = pltpu.SemaphoreType.DMA
    return pl.pallas_call(
        kernel,
        out_shape=(
            jax.ShapeDtypeStruct((1, 2, TRACES), F32),
            jax.ShapeDtypeStruct((1, 2, CMP, Q), F32),
        ),
        in_specs=[pl.BlockSpec(memory_space=pltpu.HBM)] * 5,
        out_specs=(vmem, vmem),
        scratch_shapes=[
            pltpu.VMEM((1, 2, TRACES), F32),
            pltpu.VMEM((rows, 128), jnp.int32),
            pltpu.VMEM((rows, 128), jnp.int32),
            pltpu.VMEM((rows, 128), jnp.int32),
            pltpu.VMEM((CMP, Q), F32),
            dma((5,)),
            pltpu.VMEM((128, TRACES), BF16),
            pltpu.VMEM((384, TRACES), BF16),
            pltpu.VMEM((128, 8192), BF16),
            pltpu.VMEM((320, GROUP), BF16),
            pltpu.VMEM((64, 128), jnp.int32),
            pltpu.VMEM((rows, 128), jnp.int32),
            pltpu.VMEM((BINS, Q), BF16),
            pltpu.VMEM((BINS, Q), BF16),
            pltpu.VMEM((Q, BINS), BF16),
            pltpu.VMEM((Q, BINS), BF16),
            pltpu.VMEM((CMP, BINS), F32),
            pltpu.VMEM((NU, 2, NZ, 128), F32),
            pltpu.VMEM((NU, 2, NZ, 128), F32),
            pltpu.VMEM((4, NZ, 128), F32),
            pltpu.VMEM((NZ, 8, 128), F32),
            pltpu.VMEM((NZ, 4, 128), F32),
            pltpu.VMEM((CMP, Q), F32),
            pltpu.VMEM((NF, CMP, Q), F32),
            pltpu.VMEM((NZ, NU, 128), F32),
            pltpu.VMEM((NZ, NU, 128), F32),
            pltpu.VMEM((NU, NZ, 128), F32),
            dma((NU,)), dma((NU,)), dma((NZ,)), dma((NZ,)), dma((NZ,)), dma((NZ,)),
            dma((NF,)), dma((NF,)), dma((NZ,)), dma((NZ,)), dma((NU,)), dma((NU,)),
        ],
        compiler_params=pltpu.CompilerParams(
            collective_id=0, has_side_effects=True, vmem_limit_bytes=32 * 1024 * 1024
        ),
        name="radon",
    )(
        traces,
        trace_slot.reshape(rows, 128),
        trace_cmp.reshape(rows, 128),
        trace_bin.reshape(rows, 128),
        prior_weight,
    )


def solution(mesh):
    return jax.shard_map(
        per_device,
        mesh=mesh,
        in_specs=(P("freq", None, "shot"), P("shot"), P("shot"), P("shot"), P("shot", None)),
        out_specs=(P("freq", None, "shot"), P("freq", None, "shot", None)),
        check_vma=False,
    )
```

time: 390 us -> 65.8 us (0.17); the launches traced: 382 us -> 65.3 us
  other arithmetic: 120 us -> 0 us
  local copies, waits for them, and re-layouts: 114 us -> 4.85 us
  matrix products: 65.3 us -> 0 us
  starting transfers between devices: 62.4 us -> 0 us
  Pallas kernels: 0 us -> 59.8 us
  waiting for transfers between devices: 18.6 us -> 0 us
    scatter-add x2 -> x0, other arithmetic: 89.7 us -> none  [the longest x1 46.5 us: per_device(): binned = jnp.zeros((freq_local * 2, cmp_dev * BINS + 1), jnp.float32).at[...]
    dot_general x128 -> x0, matrix products: 65.3 us -> none  [the longest x64 34 us: collect(): jnp.einsum('fcb,fqb->fcq', operand, table_part, precision=lax.Precision.H...]
    all_to_all x4 -> x0, starting transfers between devices: 62.4 us -> none  [the longest x1 21.4 us: per_device(): lax.all_to_all(returned, 'shot', split_axis=2, concat_axis=2, tiled=True)]
    pallas_call x0 -> x1, Pallas kernels: none -> 59.8 us  [per_device(): pl.pallas_call(kernel, out_shape=(jax.ShapeDtypeStruct((1, 2, TRACES), F3...]
    gather x2 -> x0, local copies, waits for them, and re-layouts: 46.4 us -> none  [the longest x1 30.1 us: per_device(): predicted[:, :, cell_index].reshape(freq_local, 2, shot_count, -1)]
    scatter x2 -> x0, local copies, waits for them, and re-layouts: 28.3 us -> none  [the longest x1 15.5 us: per_device(): jnp.zeros((slot_total,), jnp.int32).at[trace_slot]]
    all_to_all x4 -> x0, waiting for transfers between devices: 18.6 us -> none  [the longest x1 14.2 us: per_device(): lax.all_to_all(returned, 'shot', split_axis=2, concat_axis=2, tiled=True)]
    neg x1 -> x0, other arithmetic: 15.4 us -> none  [radon_table(): return (jnp.cos(phase), -jnp.sin(phase))]
  transfers between devices with their start and end apart: 4 -> 0, of which waited for: 2 -> 0; matrix products, arithmetic and copies ran while one was open for 21% -> 0% of each run, Pallas kernels for 0% -> 0%
where the time goes in v1:
time: 65.8 us; the launch traced here: 65.3 us
  Pallas kernels  59.8 us (91%)
  local copies, waits for them, and re-layouts  4.85 us (7%)
    pallas_call x1, Pallas kernels, per_device(): pl.pallas_call(kernel, out_shape=(jax.ShapeDtypeStruct((1, 2, TRACES), F3...  59.8 us
    unnamed x12, local copies, waits for them, and re-layouts  4.85 us

profile of v1, /device:TPU:1, one launch (start us, length us, event | category | flops | bytes accessed | tf_op | source)
XLA Modules:
  0.0 65.3 jit_solution(3667667700566245361)
XLA Ops:
  0.6 0.0 copy-start
  0.6 0.7 %copy-done = f32[1,2,4096]{2,1,0:T(2,128)S(1)} copy-done((f32[1,2,4096]{2,1,0:T(2,128)S(1)}, f32[1,2,4096]{2,1,0:T(2,128)}, u32[]{:S(2)}) %copy-start) | copy-done | bytes 32792
  1.4 0.0 copy-start.1
  1.4 0.7 %copy-done.1 = s32[4096]{0:T(1024)S(1)} copy-done((s32[4096]{0:T(1024)S(1)}, s32[4096]{0:T(1024)}, u32[]{:S(2)}) %copy-start.1) | copy-done | bytes 16408
  2.1 0.0 copy-start.2
  2.1 0.7 %copy-done.2 = s32[4096]{0:T(1024)S(1)} copy-done((s32[4096]{0:T(1024)S(1)}, s32[4096]{0:T(1024)}, u32[]{:S(2)}) %copy-start.2) | copy-done | bytes 16408
  2.8 0.0 copy-start.3
  2.8 0.7 %copy-done.3 = s32[4096]{0:T(1024)S(1)} copy-done((s32[4096]{0:T(1024)S(1)}, s32[4096]{0:T(1024)}, u32[]{:S(2)}) %copy-start.3) | copy-done | bytes 16408
  3.5 0.0 copy-start.4
  3.5 0.7 %copy-done.4 = f32[16,256]{1,0:T(8,128)S(1)} copy-done((f32[16,256]{1,0:T(8,128)S(1)}, f32[16,256]{1,0:T(8,128)}, u32[]{:S(2)}) %copy-start.4) | copy-done | bytes 16408
  4.3 59.8 %radon.1 = (f32[1,2,4096]{2,1,0:T(2,128)S(1)}, f32[1,2,16,256]{3,2,1,0:T(8,128)S(1)}) custom-call(f32[1,2,4096]{2,1,0:T(2,128)S(1)} %copy-done, s32[32,128]{1,0:T(8,128)S(1)} %bitcast.3, s32[32,128]{1,0:T(8,128)S(1)} %bitcast.4, s32[32,128]{1,0:T(8,128)S(1)} %bitcast.5, f32[16,256]{1,0:T(8,128)S(1)} %copy-done.4), custom_call_target="tpu_custom_call" | custom-call | tf_op jit(solution)/shard_map/radon/pallas_call | solution.py:488
  64.1 0.6 copy.9
  64.7 0.6 copy.10
Async XLA Ops:
  0.6 0.8 %copy-start = (f32[1,2,4096]{2,1,0:T(2,128)S(1)}, f32[1,2,4096]{2,1,0:T(2,128)}, u32[]{:S(2)}) copy-start(f32[1,2,4096]{2,1,0:T(2,128)} %traces_hbm.1) | copy-start | bytes 98308
  1.4 0.7 %copy-start.1 = (s32[4096]{0:T(1024)S(1)}, s32[4096]{0:T(1024)}, u32[]{:S(2)}) copy-start(s32[4096]{0:T(1024)} %param.6) | copy-start | bytes 49156
  2.1 0.7 %copy-start.2 = (s32[4096]{0:T(1024)S(1)}, s32[4096]{0:T(1024)}, u32[]{:S(2)}) copy-start(s32[4096]{0:T(1024)} %param.7) | copy-start | bytes 49156
  2.8 0.7 %copy-start.3 = (s32[4096]{0:T(1024)S(1)}, s32[4096]{0:T(1024)}, u32[]{:S(2)}) copy-start(s32[4096]{0:T(1024)} %param.8) | copy-start | bytes 49156
  3.5 0.7 %copy-start.4 = (f32[16,256]{1,0:T(8,128)S(1)}, f32[16,256]{1,0:T(8,128)}, u32[]{:S(2)}) copy-start(f32[16,256]{1,0:T(8,128)} %weight_hbm.1) | copy-start | bytes 49156

commit v2 on v1

--- a/solution.py
+++ b/solution.py
@@ -65,12 +65,12 @@
 
 
 def kernel(
-    traces_hbm, slot_hbm, cmp_hbm, bin_hbm, weight_hbm, primaries, radon_model,
-    traces, slot_in, cmp_in, bin_in, weight_in, in_sems,
+    traces_hbm, slot_hbm, cmp_hbm, bin_hbm, weight_hbm, primaries_hbm, radon_hbm,
+    traces, slot_in, cmp_in, bin_in, weight_in, in_sems, primaries, radon_model, out_sems,
     dest_hot, trace_hot, slot_low, slot_hot, row_h, row_s,
     table, table_low, table_t, table_t_low, counts_ref,
-    send_a, recv_a, pair_code, recv_v, recv_c, energy_own, energy_all, send_r, recv_r, recv_t,
-    a_send, a_recv, b_send, b_recv, c_send, c_recv, e_send, e_recv, r_send, r_recv, t_send, t_recv,
+    send_a, recv_a, send_b, recv_b, energy_own, energy_all, send_r, recv_r, recv_t,
+    a_send, a_recv, b_send, b_recv, e_send, e_recv, r_send, r_recv, t_send, t_recv,
 ):
     inputs = [
         pltpu.make_async_copy(source, target, in_sems.at[i])
@@ -119,9 +119,9 @@
         rows = pl.ds(pl.multiple_of(step * 8, 8), 8)
         slot, bins = slot_in[rows, :], bin_in[rows, :]
         dest = (((slot >> 6) & 1) * 4 + ((slot >> 7) & 3)) * NZ + (slot >> 9)
-        within = slot & 63
+        within = (slot + 16 * lax.rem(u, 4)) & 63
         row_s[rows, :] = within
-        high = (bins >> 7) * 16 + ((slot >> 4) & 3) * 4 + cmp_in[rows, :] + 1
+        high = (bins >> 7) * 4 + cmp_in[rows, :] + 1
         low = bins & 127
         high, low = high.astype(F32), low.astype(F32)
         for i in range(8):
@@ -173,28 +173,20 @@
 
     for k in range(1, NU):
         copy_a(k).wait_recv()
-    for i in range(4):
-        pair_code[i] = recv_a[i, 1] + recv_a[i + 4, 1]
-
-    def copies_b(k):
+    for i in range(NZ):
+        send_b[i, 0:8] = recv_a[:, 0, i]
+        send_b[i, 8:12] = recv_a[0:4, 1, i] + recv_a[4:8, 1, i]
+
+    def copy_b(k):
         there = lax.rem(z + k, NZ)
-        peer = {"shot": shot_of(there, u)}
-        return (
-            pltpu.make_async_remote_copy(
-                recv_a.at[:, 0, there], recv_v.at[z], b_send.at[k], b_recv.at[k],
-                device_id=peer, device_id_type=MESH,
-            ),
-            pltpu.make_async_remote_copy(
-                pair_code.at[:, there], recv_c.at[z], c_send.at[k], c_recv.at[k],
-                device_id=peer, device_id_type=MESH,
-            ),
+        return pltpu.make_async_remote_copy(
+            send_b.at[there], recv_b.at[z], b_send.at[k], b_recv.at[k],
+            device_id={"shot": shot_of(there, u)}, device_id_type=MESH,
         )
 
     for k in (8, 7, 9, 6, 10, 5, 11, 4, 12, 3, 13, 2, 14, 1, 15):
-        for copy in copies_b(k):
-            copy.start()
-    recv_v[z] = recv_a[:, 0, z]
-    recv_c[z] = pair_code[:, z]
+        copy_b(k).start()
+    recv_b[z] = send_b[z]
 
     odd_row = 2 * lax.broadcasted_iota(jnp.int32, (64, 128), 0) + 1
 
@@ -220,54 +212,69 @@
     w_plus, w_minus = weight[:, HALF:], reverse_lanes(weight[:, :HALF], flip)
 
     lane4 = lax.broadcasted_iota(jnp.int32, (4, 128), 1)
+    sub16 = lax.broadcasted_iota(jnp.int32, (16, 128), 0)
+    row8 = lax.broadcasted_iota(jnp.int32, (8, 128), 0) & 3
+    wanted = (((lane >> 4) & 3) - 2 * row8) & 3
+
+    def turn(v):
+        out = v
+        for d in range(1, 4):
+            moved = jnp.where(row8 + d < 4, pltpu.roll(v, 8 - d, 0), pltpu.roll(v, 4 - d, 0))
+            out = jnp.where(wanted == d, moved, out)
+        return out
 
     def bin_step(step, below, above, total):
         rows = pl.ds(pl.multiple_of(step * 8, 8), 8)
         re, im, code = [], [], []
         for at in (below, above):
-            first, second = recv_v[at, 0:4], recv_v[at, 4:8]
+            first, second = recv_b[at, 0:4], recv_b[at, 4:8]
             re.append(jnp.where(lane4 < 64, first, pltpu.roll(second, 64, 1)))
             im.append(jnp.where(lane4 < 64, pltpu.roll(first, 64, 1), second))
-            code.append(recv_c[at])
-        re, im = jnp.concatenate(re, axis=0), jnp.concatenate(im, axis=0)
-        code = jnp.concatenate(code, axis=0).astype(jnp.int32)
+            code.append(recv_b[at, 8:12])
+        re, im, code = (turn(jnp.concatenate(v, axis=0)) for v in (re, im, code))
+        code = code.astype(jnp.int32)
         h, low = (code >> 7) - 1, code & 127
         row_h[rows, :] = h
         pieces = [p.astype(F32) for v in (re, im) for p in split(v)]
         for i in range(8):
-            lanes = pl.ds(pl.multiple_of(step * GROUP + i * 128, 128), 128)
-            here = slice(i * 128, i * 128 + 128)
+            place = ((i % 4) * 2 + i // 4) * 128
+            lanes = pl.ds(pl.multiple_of(step * GROUP + place, 128), 128)
+            here = slice(place, place + 128)
             slot_low[:, lanes] = jnp.where(sub128 == low[i : i + 1], 1.0, 0.0).astype(BF16)
-            mask = sub64 == h[i : i + 1]
+            mask = sub16 == h[i : i + 1]
             for j, piece in enumerate(pieces):
-                slot_hot[64 * j : 64 * (j + 1), here] = jnp.where(mask, piece[i : i + 1], 0.0).astype(BF16)
-            slot_hot[256:320, here] = jnp.where(mask, 1.0, 0.0).astype(BF16)
-        lanes = pl.ds(pl.multiple_of(step * GROUP, 128), GROUP)
-        return total + mxu(slot_hot[...], slot_low[:, lanes], NT)
+                slot_hot[16 * j : 16 * (j + 1), here] = jnp.where(mask, piece[i : i + 1], 0.0).astype(BF16)
+            slot_hot[64:80, here] = jnp.where(mask, 1.0, 0.0).astype(BF16)
+        out = []
+        for quarter in range(4):
+            lanes = pl.ds(pl.multiple_of(step * GROUP + quarter * 256, 128), 256)
+            hot = slot_hot[:, quarter * 256 : quarter * 256 + 256]
+            out.append(total[quarter] + mxu(hot, slot_low[:, lanes], NT))
+        return tuple(out)
 
     def bin_pair(step, total):
         for k in (step + 1, NZ - 1 - step):
-            for copy in copies_b(k):
-                copy.wait_recv()
+            copy_b(k).wait_recv()
         return bin_step(step, lax.rem(z + NZ - 1 - step, NZ), lax.rem(z + step + 1, NZ), total)
 
-    binned = lax.fori_loop(0, 7, bin_pair, jnp.zeros((320, 128), F32))
-    for copy in copies_b(8):
-        copy.wait_recv()
+    binned = lax.fori_loop(0, 7, bin_pair, (jnp.zeros((80, 128), F32),) * 4)
+    copy_b(8).wait_recv()
     binned = bin_step(7, z, lax.rem(z + 8, NZ), binned)
 
-    def by_bin(rows):
-        return jnp.concatenate([rows[16 * i : 16 * i + 16] for i in range(4)], axis=1)
-
-    g_re = by_bin(binned[0:64] + binned[64:128])
-    g_im = by_bin(binned[128:192] + binned[192:256])
-    counts_ref[...] = by_bin(binned[256:320])
+    def by_bin(quarters):
+        return jnp.concatenate(
+            [jnp.concatenate([v[4 * i : 4 * i + 4] for i in range(4)], axis=1) for v in quarters], axis=0
+        )
+
+    g_re = by_bin([v[0:16] + v[16:32] for v in binned])
+    g_im = by_bin([v[32:48] + v[48:64] for v in binned])
+    counts_ref[...] = by_bin([v[64:80] for v in binned])
 
     def product(v, high, low):
         n = v.shape[0]
-        v_high, v_low = split(v)
-        main = mxu(jnp.concatenate([v_high, v_low], axis=0), high)
-        return main[:n] + (main[n:] + mxu(v_high, low))
+        pieces = jnp.concatenate(split(v, 3), axis=0)
+        main, rest = mxu(pieces, high), mxu(pieces[: 2 * n], low)
+        return main[:n] + ((main[n : 2 * n] + rest[:n]) + (main[2 * n :] + rest[n:]))
 
     def forward(v):
         return product(v, table_t[...], table_t_low[...])
@@ -323,22 +330,26 @@
         def cg_step(state, past, scales, own):
             answer, residual, direction, norm_now = state
             image = first_image + damp(direction) if own and not past else image_of(direction)
-            step_size = both_parts(norm_now / inner(direction, image))
+            step = norm_now / inner(direction, image)
+            coming = norm_now + step * (step * inner(image, image) - 2.0 * inner(residual, image))
+            ratio = jnp.maximum(coming, 0.0) / norm_now
             kept = project(image, past, scales)
             if own:
                 swapped = swap(residual)
                 kept = kept - both_parts(inner(swapped, image) / norm_now) * swapped
-            answer = answer + step_size * direction
-            residual = residual - step_size * kept
+            answer = answer + both_parts(step) * direction
+            residual = residual - both_parts(step) * kept
             norm_next = inner(residual, residual)
-            direction = residual + both_parts(norm_next / norm_now) * direction
+            if not past:
+                ratio = norm_next / norm_now
+            direction = residual + both_parts(ratio) * direction
             return answer, residual, direction, norm_next
 
         state = (jnp.zeros_like(right_side), right_side, right_side, inner(right_side, right_side))
         past, scales = [], []
         for _ in range(KEPT):
             residual, norm = state[1], state[3]
-            state = cg_step(state, past, scales, True)
+            state = cg_step(state, tuple(past), scales, True)
             past.append(residual)
             scales.append(1.0 / norm)
         state = lax.fori_loop(
@@ -391,7 +402,13 @@
     p_re = shift_cos * field[:CMP] + shift_sin * field[CMP:]
     p_im = shift_cos * field[CMP:] - shift_sin * field[:CMP]
     predicted = jnp.concatenate(
-        [p[:, 128 * i : 128 * i + 128] for p in (p_re, p_im) for i in range(4)], axis=0
+        [
+            p[4 * quarter : 4 * quarter + 4, 128 * i : 128 * i + 128]
+            for quarter in range(4)
+            for p in (p_re, p_im)
+            for i in range(4)
+        ],
+        axis=0,
     )
     predicted = jnp.concatenate(split(predicted), axis=1)
 
@@ -406,16 +423,19 @@
 
     def predict(step, below, above):
         rows = pl.ds(pl.multiple_of(step * 8, 8), 8)
-        low = slot_low[:, pl.ds(pl.multiple_of(step * GROUP, 128), GROUP)]
-        found = mxu(predicted, jnp.concatenate([low, low], axis=0))
         h = row_h[rows, :]
-        got_re, got_im = [], []
-        for i in range(8):
-            mask = sub64 == h[i : i + 1]
-            here = slice(i * 128, i * 128 + 128)
-            got_re.append(jnp.sum(jnp.where(mask, found[:64, here], 0.0), axis=0, keepdims=True))
-            got_im.append(jnp.sum(jnp.where(mask, found[64:, here], 0.0), axis=0, keepdims=True))
-        got_re, got_im = jnp.concatenate(got_re, axis=0), jnp.concatenate(got_im, axis=0)
+        got_re, got_im = [None] * 8, [None] * 8
+        for quarter in range(4):
+            low = slot_low[:, pl.ds(pl.multiple_of(step * GROUP + quarter * 256, 128), 256)]
+            mine = predicted[32 * quarter : 32 * quarter + 32]
+            found = mxu(mine, jnp.concatenate([low, low], axis=0))
+            for part in range(2):
+                i = part * 4 + quarter
+                mask = sub16 == h[i : i + 1]
+                here = slice(part * 128, part * 128 + 128)
+                got_re[i] = jnp.sum(jnp.where(mask, found[:16, here], 0.0), axis=0, keepdims=True)
+                got_im[i] = jnp.sum(jnp.where(mask, found[16:, here], 0.0), axis=0, keepdims=True)
+        got_re, got_im = turn(jnp.concatenate(got_re, axis=0)), turn(jnp.concatenate(got_im, axis=0))
         first = jnp.where(lane8 < 64, got_re, pltpu.roll(got_im, 64, 1))
         second = jnp.where(lane8 < 64, pltpu.roll(got_re, 64, 1), got_im)
         for i, at in enumerate((below, above)):
@@ -436,6 +456,8 @@
     for part in range(2):
         radon_model[0, part, :, 0:HALF] = reverse_lanes(minus[part], flip)
         radon_model[0, part, :, HALF:Q] = plus[part]
+    model_out = pltpu.make_async_copy(radon_model, radon_hbm, out_sems.at[0])
+    model_out.start()
 
     for k in range(1, NZ):
         copy_r(k).wait_recv()
@@ -452,6 +474,12 @@
     recv_t[u] = recv_r[:, u]
     for k in range(1, NU):
         copy_t(k).wait_recv()
+
+    def part_out(step):
+        lanes = pl.ds(pl.multiple_of(step * GROUP, 128), GROUP)
+        return pltpu.make_async_copy(
+            primaries.at[:, :, lanes], primaries_hbm.at[:, :, lanes], out_sems.at[1 + step]
+        )
 
     by_slot = jnp.concatenate(split(recv_t[...].reshape(128, 128).T), axis=1)
 
@@ -469,21 +497,24 @@
             primaries[0, 0:1, lanes] = traces[0, 0:1, lanes] - got
             got = jnp.sum(jnp.where(mask, found[64:, here], 0.0), axis=0, keepdims=True)
             primaries[0, 1:2, lanes] = traces[0, 1:2, lanes] - got
+        part_out(step).start()
 
     for k in range(1, NU):
         copy_a(k).wait_send()
         copy_t(k).wait_send()
     for k in range(1, NZ):
-        for copy in copies_b(k):
-            copy.wait_send()
+        copy_b(k).wait_send()
         copy_r(k).wait_send()
     for k in range(1, NF):
         copy_e(k).wait_send()
+    model_out.wait()
+    for step in range(TRACES // GROUP):
+        part_out(step).wait()
 
 
 def per_device(traces, trace_slot, trace_cmp, trace_bin, prior_weight):
     rows = TRACES // 128
-    vmem = pl.BlockSpec(memory_space=pltpu.VMEM)
+    hbm = pl.BlockSpec(memory_space=pltpu.HBM)
     dma = pltpu.SemaphoreType.DMA
     return pl.pallas_call(
         kernel,
@@ -491,8 +522,8 @@
             jax.ShapeDtypeStruct((1, 2, TRACES), F32),
             jax.ShapeDtypeStruct((1, 2, CMP, Q), F32),
         ),
-        in_specs=[pl.BlockSpec(memory_space=pltpu.HBM)] * 5,
-        out_specs=(vmem, vmem),
+        in_specs=[hbm] * 5,
+        out_specs=(hbm, hbm),
         scratch_shapes=[
             pltpu.VMEM((1, 2, TRACES), F32),
             pltpu.VMEM((rows, 128), jnp.int32),
@@ -500,10 +531,13 @@
             pltpu.VMEM((rows, 128), jnp.int32),
             pltpu.VMEM((CMP, Q), F32),
             dma((5,)),
+            pltpu.VMEM((1, 2, TRACES), F32),
+            pltpu.VMEM((1, 2, CMP, Q), F32),
+            dma((1 + TRACES // GROUP,)),
             pltpu.VMEM((128, TRACES), BF16),
             pltpu.VMEM((384, TRACES), BF16),
             pltpu.VMEM((128, 8192), BF16),
-            pltpu.VMEM((320, GROUP), BF16),
+            pltpu.VMEM((80, GROUP), BF16),
             pltpu.VMEM((64, 128), jnp.int32),
             pltpu.VMEM((rows, 128), jnp.int32),
             pltpu.VMEM((BINS, Q), BF16),
@@ -513,19 +547,18 @@
             pltpu.VMEM((CMP, BINS), F32),
             pltpu.VMEM((NU, 2, NZ, 128), F32),
             pltpu.VMEM((NU, 2, NZ, 128), F32),
-            pltpu.VMEM((4, NZ, 128), F32),
-            pltpu.VMEM((NZ, 8, 128), F32),
-            pltpu.VMEM((NZ, 4, 128), F32),
+            pltpu.VMEM((NZ, 12, 128), F32),
+            pltpu.VMEM((NZ, 12, 128), F32),
             pltpu.VMEM((CMP, Q), F32),
             pltpu.VMEM((NF, CMP, Q), F32),
             pltpu.VMEM((NZ, NU, 128), F32),
             pltpu.VMEM((NZ, NU, 128), F32),
             pltpu.VMEM((NU, NZ, 128), F32),
-            dma((NU,)), dma((NU,)), dma((NZ,)), dma((NZ,)), dma((NZ,)), dma((NZ,)),
+            dma((NU,)), dma((NU,)), dma((NZ,)), dma((NZ,)),
             dma((NF,)), dma((NF,)), dma((NZ,)), dma((NZ,)), dma((NU,)), dma((NU,)),
         ],
         compiler_params=pltpu.CompilerParams(
-            collective_id=0, has_side_effects=True, vmem_limit_bytes=32 * 1024 * 1024
+            collective_id=0, has_side_effects=True, vmem_limit_bytes=56 * 1024 * 1024
         ),
         name="radon",
     )(

time: 65.8 us -> 61.4 us (0.933)
  local copies, waits for them, and re-layouts: 4.85 us -> 2 us
  Pallas kernels: 59.8 us -> 58.4 us
    unnamed x12 -> x4, local copies, waits for them, and re-layouts: 4.85 us -> 2 us
    pallas_call x1, Pallas kernels: 59.8 us -> 58.4 us  [per_device(): pl.pallas_call(kernel, out_shape=(jax.ShapeDtypeStruct((1, 2, TRACES), F3...]
where the time goes in v2:
time: 61.4 us; the launch traced here: 61.1 us
  Pallas kernels  58.4 us (95%)
  local copies, waits for them, and re-layouts  2 us (3%)
  between operations  0.65 us (1%)
    pallas_call x1, Pallas kernels, per_device(): pl.pallas_call(kernel, out_shape=(jax.ShapeDtypeStruct((1, 2, TRACES), F3...  58.4 us
    unnamed x4, local copies, waits for them, and re-layouts  2 us

profile of v2, /device:TPU:1, one launch (start us, length us, event | category | flops | bytes accessed | tf_op | source)
XLA Modules:
  0.0 61.1 jit_solution(17958965135218646910)
XLA Ops:
  0.6 58.4 %radon.1 = (f32[1,2,4096]{2,1,0:T(2,128)}, f32[1,2,16,256]{3,2,1,0:T(8,128)}) custom-call(f32[1,2,4096]{2,1,0:T(2,128)} %traces_hbm.1, s32[32,128]{1,0:T(8,128)} %bitcast.3, s32[32,128]{1,0:T(8,128)} %bitcast.4, s32[32,128]{1,0:T(8,128)} %bitcast.5, f32[16,256]{1,0:T(8,128)} %weight_hbm.1), custom_call_target="tpu_custom_call" | custom-call | tf_op jit(solution)/shard_map/radon/pallas_call | solution.py:519
  59.1 0.0 copy-start
  59.1 1.4 %copy.9 = f32[1,2,4096]{2,1,0:T(2,128)} copy(f32[1,2,4096]{2,1,0:T(2,128)} %get-tuple-element.4) | data formatting | bytes 65536
  60.5 0.0 copy-done
  60.5 0.6 %copy.10 = f32[1,2,16,256]{3,2,1,0:T(8,128)} copy(f32[1,2,16,256]{3,2,1,0:T(8,128)S(1)} %copy-done) | data formatting | bytes 65536
Async XLA Ops:
  59.1 1.4 %copy-start = (f32[1,2,16,256]{3,2,1,0:T(8,128)S(1)}, f32[1,2,16,256]{3,2,1,0:T(8,128)}, u32[]{:S(2)}) copy-start(f32[1,2,16,256]{3,2,1,0:T(8,128)} %get-tuple-element.5) | copy-start | bytes 98308

commit v3 on v2

--- a/solution.py
+++ b/solution.py
@@ -114,7 +114,7 @@
     for copy in inputs:
         copy.wait()
 
-    @pl.loop(0, TRACES // GROUP)
+    @pl.loop(0, TRACES // GROUP, unroll=True)
     def _(step):
         rows = pl.ds(pl.multiple_of(step * 8, 8), 8)
         slot, bins = slot_in[rows, :], bin_in[rows, :]
@@ -352,9 +352,8 @@
             state = cg_step(state, tuple(past), scales, True)
             past.append(residual)
             scales.append(1.0 / norm)
-        state = lax.fori_loop(
-            KEPT, CG_STEPS - 1, lambda _, state: cg_step(state, past, scales, False), state
-        )
+        for _ in range(KEPT, CG_STEPS - 1):
+            state = cg_step(state, past, scales, False)
         answer, _, direction, norm_now = state
         return answer + both_parts(norm_now / inner(direction, image_of(direction))) * direction
 
@@ -446,7 +445,7 @@
     copy_r(8).start()
     recv_r[z] = send_r[z]
 
-    @pl.loop(0, 7)
+    @pl.loop(0, 7, unroll=True)
     def _(back):
         step = 6 - back
         predict(step, lax.rem(z + NZ - 1 - step, NZ), lax.rem(z + step + 1, NZ))
@@ -483,7 +482,7 @@
 
     by_slot = jnp.concatenate(split(recv_t[...].reshape(128, 128).T), axis=1)
 
-    @pl.loop(0, TRACES // GROUP)
+    @pl.loop(0, TRACES // GROUP, unroll=True)
     def _(step):
         rows = pl.ds(pl.multiple_of(step * 8, 8), 8)
         hot = dest_hot[:, pl.ds(pl.multiple_of(step * GROUP, 128), GROUP)]

time: 61.4 us -> 59.3 us (0.966)
  Pallas kernels: 58.4 us -> 56.4 us
    pallas_call x1, Pallas kernels: 58.4 us -> 56.4 us  [per_device(): pl.pallas_call(kernel, out_shape=(jax.ShapeDtypeStruct((1, 2, TRACES), F3...]
where the time goes in v3:
time: 59.3 us; the launch traced here: 59 us
  Pallas kernels  56.4 us (95%)
  local copies, waits for them, and re-layouts  2 us (3%)
  between operations  0.65 us (1%)
    pallas_call x1, Pallas kernels, per_device(): pl.pallas_call(kernel, out_shape=(jax.ShapeDtypeStruct((1, 2, TRACES), F3...  56.4 us
    unnamed x4, local copies, waits for them, and re-layouts  2 us

profile of v3, /device:TPU:1, one launch (start us, length us, event | category | flops | bytes accessed | tf_op | source)
XLA Modules:
  0.0 59.0 jit_solution(2012227935882344033)
XLA Ops:
  0.6 56.4 %radon.1 = (f32[1,2,4096]{2,1,0:T(2,128)}, f32[1,2,16,256]{3,2,1,0:T(8,128)}) custom-call(f32[1,2,4096]{2,1,0:T(2,128)} %traces_hbm.1, s32[32,128]{1,0:T(8,128)} %bitcast.3, s32[32,128]{1,0:T(8,128)} %bitcast.4, s32[32,128]{1,0:T(8,128)} %bitcast.5, f32[16,256]{1,0:T(8,128)} %weight_hbm.1), custom_call_target="tpu_custom_call" | custom-call | tf_op jit(solution)/shard_map/radon/pallas_call | solution.py:518
  57.0 0.0 copy-start
  57.0 1.4 %copy.9 = f32[1,2,4096]{2,1,0:T(2,128)} copy(f32[1,2,4096]{2,1,0:T(2,128)} %get-tuple-element.4) | data formatting | bytes 65536
  58.4 0.0 copy-done
  58.4 0.6 %copy.10 = f32[1,2,16,256]{3,2,1,0:T(8,128)} copy(f32[1,2,16,256]{3,2,1,0:T(8,128)S(1)} %copy-done) | data formatting | bytes 65536
Async XLA Ops:
  57.0 1.4 %copy-start = (f32[1,2,16,256]{3,2,1,0:T(8,128)S(1)}, f32[1,2,16,256]{3,2,1,0:T(8,128)}, u32[]{:S(2)}) copy-start(f32[1,2,16,256]{3,2,1,0:T(8,128)} %get-tuple-element.5) | copy-start | bytes 98308

commit v4 on v3

--- a/solution.py
+++ b/solution.py
@@ -257,7 +257,7 @@
             copy_b(k).wait_recv()
         return bin_step(step, lax.rem(z + NZ - 1 - step, NZ), lax.rem(z + step + 1, NZ), total)
 
-    binned = lax.fori_loop(0, 7, bin_pair, (jnp.zeros((80, 128), F32),) * 4)
+    binned = lax.fori_loop(0, 7, bin_pair, (jnp.zeros((80, 128), F32),) * 4, unroll=True)
     copy_b(8).wait_recv()
     binned = bin_step(7, z, lax.rem(z + 8, NZ), binned)
 
@@ -458,6 +458,12 @@
     model_out = pltpu.make_async_copy(radon_model, radon_hbm, out_sems.at[0])
     model_out.start()
 
+    for k in range(1, NU):
+        copy_a(k).wait_send()
+    for k in range(1, NZ):
+        copy_b(k).wait_send()
+    for k in range(1, NF):
+        copy_e(k).wait_send()
     for k in range(1, NZ):
         copy_r(k).wait_recv()
 
@@ -471,6 +477,8 @@
     for k in range(1, NU):
         copy_t(k).start()
     recv_t[u] = recv_r[:, u]
+    for k in range(1, NZ):
+        copy_r(k).wait_send()
     for k in range(1, NU):
         copy_t(k).wait_recv()
 
@@ -499,13 +507,7 @@
         part_out(step).start()
 
     for k in range(1, NU):
-        copy_a(k).wait_send()
         copy_t(k).wait_send()
-    for k in range(1, NZ):
-        copy_b(k).wait_send()
-        copy_r(k).wait_send()
-    for k in range(1, NF):
-        copy_e(k).wait_send()
     model_out.wait()
     for step in range(TRACES // GROUP):
         part_out(step).wait()

time: 59.3 us -> 59.2 us (level)
  no operation moved by 1% of the time
where the time goes in v4:
time: 59.2 us; the launch traced here: 58.9 us
  Pallas kernels  56.2 us (95%)
  local copies, waits for them, and re-layouts  2 us (3%)
  between operations  0.65 us (1%)
    pallas_call x1, Pallas kernels, per_device(): pl.pallas_call(kernel, out_shape=(jax.ShapeDtypeStruct((1, 2, TRACES), F3...  56.2 us
    unnamed x4, local copies, waits for them, and re-layouts  2 us

profile of v4, /device:TPU:1, one launch (start us, length us, event | category | flops | bytes accessed | tf_op | source)
XLA Modules:
  0.0 58.9 jit_solution(17151752971238186197)
XLA Ops:
  0.6 56.2 %radon.1 = (f32[1,2,4096]{2,1,0:T(2,128)}, f32[1,2,16,256]{3,2,1,0:T(8,128)}) custom-call(f32[1,2,4096]{2,1,0:T(2,128)} %traces_hbm.1, s32[32,128]{1,0:T(8,128)} %bitcast.3, s32[32,128]{1,0:T(8,128)} %bitcast.4, s32[32,128]{1,0:T(8,128)} %bitcast.5, f32[16,256]{1,0:T(8,128)} %weight_hbm.1), custom_call_target="tpu_custom_call" | custom-call | tf_op jit(solution)/shard_map/radon/pallas_call | solution.py:520
  56.9 0.0 copy-start
  56.9 1.4 %copy.9 = f32[1,2,4096]{2,1,0:T(2,128)} copy(f32[1,2,4096]{2,1,0:T(2,128)} %get-tuple-element.4) | data formatting | bytes 65536
  58.3 0.0 copy-done
  58.3 0.6 %copy.10 = f32[1,2,16,256]{3,2,1,0:T(8,128)} copy(f32[1,2,16,256]{3,2,1,0:T(8,128)S(1)} %copy-done) | data formatting | bytes 65536
Async XLA Ops:
  56.9 1.4 %copy-start = (f32[1,2,16,256]{3,2,1,0:T(8,128)S(1)}, f32[1,2,16,256]{3,2,1,0:T(8,128)}, u32[]{:S(2)}) copy-start(f32[1,2,16,256]{3,2,1,0:T(8,128)} %get-tuple-element.5) | copy-start | bytes 98308
